TPU v7x, 256 devices: a whole 4x4x8 slice. The times are simulated.
256 devices in a mesh: cont: 8 (over z), line: 8 (over y, core), scen: 4 (over x).
Axes of the slice: x: 4, y: 4, z: 8, core: 2. Of those that a mesh axis runs over, the one named last changes fastest.
Arguments:
- lodf: bfloat16 [1024, 4096], P('line', 'cont'), may hold values from -1 to 1
- flow: float32 [1024, 256], P('line', 'scen'), may hold values from -6 to 6
- out_flow: float32 [256, 4096], P('scen', 'cont'), may hold values from -6 to 6
- limits: float32 [1024], P('line'), may hold values from 0.5 to 2
- ptdf_mon: bfloat16 [1024, 2048], P('line'), may hold values from -6 to 6
- ptdf_out: bfloat16 [4096, 2048], P('cont'), may hold values from -6 to 6
- viol_cont: int32 [131072], P(('cont', 'line', 'scen')), may hold values from 0 to 511
- viol_line: int32 [131072], P(('cont', 'line', 'scen')), may hold values from 0 to 127
- viol_scen: int32 [131072], P(('cont', 'line', 'scen')), may hold values from 0 to 63
- rows_used: int32 [256], P(('cont', 'line', 'scen')), may hold values from 64 to 512, as said below
Outputs:
- worst: float32 [1024, 256], P('line', 'scen')
- schur: float32 [2048, 2048], P(('line', 'scen'))
Inputs may be any that keep to these rules, and one draw needn't show every extreme that they name: `rows_used`: each device uses a leading run of its 512 slots; the counts are skewed, and some device is full.
All inputs are finite; a program needn't handle non-finite values.
Results may differ from a plain program's by a relative error of at most 0.00096.
Values may be sent and summed in bfloat16 or wider, within the bound.
No kernel may reach another device: no remote copies, remote signals or barrier semaphores. Data moves between devices by JAX's collectives and lax.ppermute only.
A program may use at most 128 MiB of HBM per device.

v0:
```python
import math
import jax
import jax.numpy as jnp
from jax import lax
from jax.sharding import PartitionSpec as P


def local(
    lodf, flow, out_flow, limits, ptdf_mon, ptdf_out, viol_cont, viol_line, viol_scen, rows_used
):
    line_dev, cont_dev = lodf.shape
    scen_dev = flow.shape[1]
    width = ptdf_mon.shape[1]
    n_rows = viol_cont.shape[0]
    n_cont = lax.axis_size("cont")
    n_line = lax.axis_size("line")
    n_scen = lax.axis_size("scen")
    owners = n_line * n_scen
    devices = n_cont * owners
    row_block = math.gcd(n_rows, 512)
    lines_each = math.gcd(line_dev, 32)

    def screen(pair):
        lodf_block, flow_block = pair
        post = (
            flow_block[:, :, None]
            + lodf_block.astype(jnp.float32)[:, None, :] * out_flow[None, :, :]
        )
        return jnp.max(jnp.abs(post), axis=2)

    local_worst = lax.map(
        screen,
        (
            lodf.reshape(line_dev // lines_each, lines_each, cont_dev),
            flow.reshape(line_dev // lines_each, lines_each, scen_dev),
        ),
    ).reshape(line_dev, scen_dev)
    worst = lax.pmax(local_worst, "cont") / limits[:, None]
    coef = lodf[viol_line, viol_cont].astype(jnp.float32)
    rows = (
        ptdf_mon[viol_line].astype(jnp.float32)
        + coef[:, None] * ptdf_out[viol_cont].astype(jnp.float32)
    ).astype(jnp.bfloat16)
    rows = lax.optimization_barrier(rows)
    post = flow[viol_line, viol_scen] + coef * out_flow[viol_scen, viol_cont]
    ratio = post / limits[viol_line]
    live = jnp.arange(n_rows, dtype=jnp.int32) < rows_used[0]
    weight = jnp.where(live, 1.0 + ratio * ratio, jnp.zeros_like(ratio))
    scaled = (weight[:, None] * rows.astype(jnp.float32)).astype(jnp.bfloat16)
    trips = (rows_used[0] + row_block - 1) // row_block
    row_blocks = rows.reshape(n_rows // row_block, row_block, width)
    scaled_blocks = scaled.reshape(n_rows // row_block, row_block, width)

    def step(index, acc):
        row_tile = lax.dynamic_index_in_dim(row_blocks, index, 0, keepdims=False)
        scaled_tile = lax.dynamic_index_in_dim(scaled_blocks, index, 0, keepdims=False)
        return acc + lax.dot_general(
            row_tile, scaled_tile, (((0,), (0,)), ((), ())), preferred_element_type=jnp.float32
        )

    owned = lax.psum_scatter(
        lax.fori_loop(
            0,
            trips,
            step,
            jnp.zeros((lax.axis_size(("line", "scen")) * (width // owners), width), jnp.float32),
        ),
        ("line", "scen"),
        scatter_dimension=0,
        tiled=True,
    )
    total = lax.psum(owned, "cont")
    schur = total * (1.0 / (n_rows * devices))
    return (worst, schur)


def solution(mesh):
    in_specs = (
        P("line", "cont"),
        P("line", "scen"),
        P("scen", "cont"),
        P("line"),
        P("line", None),
        P("cont", None),
        P(("cont", "line", "scen")),
        P(("cont", "line", "scen")),
        P(("cont", "line", "scen")),
        P(("cont", "line", "scen")),
    )
    out_specs = (P("line", "scen"), P(("line", "scen"), None))
    return jax.shard_map(local, mesh=mesh, in_specs=in_specs, out_specs=out_specs, check_vma=False)
```

profile of v0, /device:TPU:2, one launch (start us, length us, event | category | flops | bytes accessed | tf_op | source)
XLA Modules:
  0.0 275.0 jit_solution(17831814919024099587)
XLA Ops:
  8.8 5.2 %gather_fusion.1 = bf16[512]{0:T(512)(128)(2,1)S(1)} fusion(bf16[128,512]{1,0:T(8,128)(2,1)} %param.14, s32[512]{0:T(512)S(1)} %get-tuple-element.84), kind=kCustom, calls=%fused_computation.1 | custom fusion | bytes 6144 | tf_op jit(solution)/shard_map/gather | solution.py:39
  14.0 3.3 %gather_fusion = bf16[512,2048]{1,0:T(8,128)(2,1)} fusion(bf16[128,2048]{1,0:T(8,128)(2,1)S(1)} %copy-done.2, s32[1024]{0:T(1024)S(1)} %get-tuple-element.89), kind=kCustom, calls=%fused_computation | custom fusion | bytes 4196352 | tf_op jit(solution)/shard_map/gather | solution.py:41
  17.3 3.3 %gather_fusion.2 = bf16[512,2048]{1,0:T(8,128)(2,1)} fusion(bf16[512,2048]{1,0:T(8,128)(2,1)S(1)} %copy-done, s32[1024]{0:T(1024)S(1)} %get-tuple-element.88), kind=kCustom, calls=%fused_computation.2 | custom fusion | bytes 4196352 | tf_op jit(solution)/shard_map/gather | solution.py:42
  20.6 4.2 %add_convert_fusion = bf16[512,2048]{1,0:T(8,128)(2,1)} fusion(bf16[512,2048]{1,0:T(8,128)(2,1)} %gather_fusion.2, bf16[512,2048]{1,0:T(8,128)(2,1)} %gather_fusion, f32[512]{0:T(512)S(1)} %convert_element_type.36), kind=kLoop, calls=%fused_computation.14 | loop fusion | flops 5242880 | bytes 6293504 | tf_op jit(solution)/shard_map/convert_element_type | solution.py:43
  24.8 3.3 %gather_fusion.5 = f32[512]{0:T(512)S(1)} fusion(f32[128]{0:T(128)S(1)} %copy-done.1, s32[1024]{0:T(1024)S(1)} %get-tuple-element.89), kind=kCustom, calls=%fused_computation.5 | custom fusion | bytes 6144 | tf_op jit(solution)/shard_map/gather | solution.py:46
  28.2 3.7 %gather_fusion.3 = f32[512]{0:T(512)S(1)} fusion(f32[128,64]{0,1:T(8,128)S(1)} %copy-done.3, s32[512]{0:T(512)S(1)} %get-tuple-element.85), kind=kCustom, calls=%fused_computation.3 | custom fusion | bytes 8192 | tf_op jit(solution)/shard_map/gather | solution.py:45
  32.0 4.5 %gather_fusion.4 = f32[512]{0:T(512)S(1)} fusion(f32[64,512]{1,0:T(8,128)S(1)} %copy-done.4, s32[512]{0:T(512)S(1)} %get-tuple-element.83), kind=kCustom, calls=%fused_computation.4 | custom fusion | bytes 8192 | tf_op jit(solution)/shard_map/gather | solution.py:45
  36.5 3.3 %fusion.2 = bf16[1,512,2048]{2,1,0:T(8,128)(2,1)} fusion(bf16[512,2048]{1,0:T(8,128)(2,1)} %add_convert_fusion, f32[512]{0:T(512)S(1)} %add_select_fusion), kind=kLoop, calls=%fused_computation.15 | loop fusion | flops 3145728 | bytes 4196352 | tf_op jit(solution)/shard_map/reshape | solution.py:52
  39.8 7.9 %broadcast_in_dim.20 = f32[2048,2048]{1,0:T(8,128)} broadcast(f32[]{:T(128)} %constant.46.clone.1), dimensions={} | broadcast | bytes 16777220 | tf_op jit(solution)/shard_map/broadcast_in_dim | solution.py:66
  47.7 17.3 %while.21 = (s32[]{:T(128)}, f32[2048,2048]{1,0:T(8,128)}, s32[]{:T(128)}, bf16[1,512,2048]{2,1,0:T(8,128)(2,1)}, bf16[1,512,2048]{2,1,0:T(8,128)(2,1)}, /*index=5*/s32[]{:T(128)}) while((s32[]{:T(128)}, f32[2048,2048]{1,0:T(8,128)}, s32[]{:T(128)}, bf16[1,512,2048]{2,1,0:T(8,128)(2,1)}, bf16[1,512,2048]{2,1,0:T(8,128)(2,1)}, ...), condition=%wide.region_5.6_spmd, body=%wide.region_4.5_spmd.sunk | while | flops 4299161600 | bytes 37748804 | solution.py:62
  47.7 17.3 %convolution_add_fusion.2 = f32[2048,2048]{1,0:T(8,128)} fusion(f32[2048,2048]{1,0:T(8,128)} %get-tuple-element.178, bf16[1,512,2048]{2,1,0:T(8,128)(2,1)} %get-tuple-element.187, bf16[1,512,2048]{2,1,0:T(8,128)(2,1)} %get-tuple-element.186), kind=kOutput, calls=%fused_computation.10.clone.1 | convolution fusion | flops 4299161600 | bytes 37748736 | tf_op jit(solution)/shard_map/while/body/dot_general | solution.py:57
  65.2 125.7 %reduce-scatter.2.cloned.1.call-done = f32[64,2048]{1,0:T(8,128)} async-done(((f32[2048,2048]{1,0:T(8,128)}), f32[64,2048]{1,0:T(8,128)}) %reduce-scatter.2.cloned.1.call-update) | async-done | bytes 524304 | tf_op jit(solution)/shard_map/reduce_scatter | solution.py:61
  191.0 7.2 %while.20 = (s32[]{:T(128)}, f32[4,32,64]{2,1,0:T(8,128)S(1)}, f32[4,32,64]{2,1,0:T(8,128)S(1)}, bf16[4,32,512]{2,1,0:T(8,128)(2,1)}, f32[64,512]{1,0:T(8,128)S(1)}, /*index=5*/s32[]{:T(128)}) while((s32[]{:T(128)}, f32[4,32,64]{2,1,0:T(8,128)S(1)}, f32[4,32,64]{2,1,0:T(8,128)S(1)}, bf16[4,32,512]{2,1,0:T(8,128)(2,1)}, ...), condition=%wide.region_2.3_spmd, body=%wide.region_0.2_spmd.sunk | while | flops 4208642 | bytes 360529 | solution.py:31
  191.0 0.8 bitcast_convert_fusion.2
  191.8 1.0 abs_reduce_fusion.2
  192.8 0.8 bitcast_convert_fusion.2
  193.6 1.0 abs_reduce_fusion.2
  194.6 0.8 bitcast_convert_fusion.2
  195.4 1.0 abs_reduce_fusion.2
  196.4 0.8 bitcast_convert_fusion.2
  197.2 1.0 abs_reduce_fusion.2
  198.2 30.7 %pmax.7 = f32[128,64]{1,0:T(8,128)S(1)} all-reduce(f32[128,64]{1,0:T(8,128)S(1)} %bitcast.35), channel_id=1, replica_groups=mesh['cont'=8,'line'=8,'scen'=4] {'cont'}, use_global_device_ids=true, to_apply=%region_3.4 | all-reduce | flops 8192 | bytes 65536 | tf_op jit(solution)/shard_map/pmax | solution.py:38
  229.7 36.6 %all-reduce.2.cloned.1.call-done = f32[64,2048]{1,0:T(8,128)} async-done(((f32[64,2048]{1,0:T(8,128)}), f32[64,2048]{1,0:T(8,128)}) %all-reduce.2.cloned.1.call-update) | async-done | bytes 524304 | tf_op jit(solution)/shard_map/psum | solution.py:72
  266.3 1.9 broadcast_multiply_fusion
  (30 shorter events, 1.8 us)
Async XLA Ops:
  7.2 10.1 %copy-start = (bf16[512,2048]{1,0:T(8,128)(2,1)S(1)}, bf16[512,2048]{1,0:T(8,128)(2,1)}, u32[]{:S(2)}) copy-start(bf16[512,2048]{1,0:T(8,128)(2,1)} %param.19) | copy-start | bytes 6291460
  7.2 6.8 %copy-start.2 = (bf16[128,2048]{1,0:T(8,128)(2,1)S(1)}, bf16[128,2048]{1,0:T(8,128)(2,1)}, u32[]{:S(2)}) copy-start(bf16[128,2048]{1,0:T(8,128)(2,1)} %param.18) | copy-start | bytes 1572868
  7.2 183.8 %reduce-scatter.2.cloned.1.call-start = ((), (), s32[]{:S(2)}) async-start(), calls=%async_computation.1 | async-start | bytes 17301504 | tf_op jit(solution)/shard_map/reduce_scatter | solution.py:61
  20.6 4.2 %copy-start.1 = (f32[128]{0:T(128)S(1)}, f32[128]{0:T(128)}, u32[]{:S(2)}) copy-start(f32[128]{0:T(128)} %param.17) | copy-start | bytes 1540
  24.8 3.4 %copy-start.3 = (f32[128,64]{0,1:T(8,128)S(1)}, f32[128,64]{0,1:T(8,128)}, u32[]{:S(2)}) copy-start(f32[128,64]{0,1:T(8,128)} %param.15) | copy-start | bytes 98308
  24.8 7.1 %copy-start.4 = (f32[64,512]{1,0:T(8,128)S(1)}, f32[64,512]{1,0:T(8,128)}, u32[]{:S(2)}) copy-start(f32[64,512]{1,0:T(8,128)} %param.16) | copy-start | bytes 393220
  65.1 201.2 %all-reduce.2.cloned.1.call-start = ((), (), s32[]{:S(2)}) async-start(), calls=%async_computation.2 | async-start | bytes 1048576 | tf_op jit(solution)/shard_map/psum | solution.py:72
Sparse Core Ops, SparseCore 0:
  65.2 125.7 reduce-scatter.1
  193.3 72.9 all-reduce.1
where the time goes:
time: 276 us; the launch traced here: 275 us
  waiting for transfers between devices  162 us (59%)
  local copies, waits for them, and re-layouts  32.1 us (12%)
  blocking collectives  30.7 us (11%)
  other arithmetic  17.3 us (6%)
  matrix products  17.3 us (6%)
  between operations  15 us (5%)
    reduce_scatter x1, waiting for transfers between devices, local(): lax.psum_scatter(lax.fori_loop(0, trips, step, jnp.zeros((lax.axis_size((...  126 us
    psum x1, waiting for transfers between devices, local(): total = lax.psum(owned, 'cont')  36.6 us
    pmax x1, blocking collectives, local(): worst = lax.pmax(local_worst, 'cont') / limits[:, None]  30.7 us
    dot_general x1, matrix products, step(): lax.dot_general(row_tile, scaled_tile, (((0,), (0,)), ((), ())), preferre...  17.3 us
    gather x2, local copies, waits for them, and re-layouts, local(): post = flow[viol_line, viol_scen] + coef * out_flow[viol_scen, viol_cont]  8.27 us
    broadcast_in_dim x1, local copies, waits for them, and re-layouts, local(): jnp.zeros((lax.axis_size(('line', 'scen')) * (width // owners), width), j...  7.86 us
  transfers between devices with their start and end apart: 2, of which 2 were waited for; matrix products, arithmetic and copies ran while one was open for 3% of the time, Pallas kernels for 0%

commit v1 on v0

--- a/solution.py
+++ b/solution.py
@@ -69,7 +69,9 @@
         scatter_dimension=0,
         tiled=True,
     )
-    total = lax.psum(owned, "cont")
+    total = owned
+    for hop in (1, 2, 4):
+        total = total + lax.ppermute(total, "cont", [(dev, dev ^ hop) for dev in range(8)])
     schur = total * (1.0 / (n_rows * devices))
     return (worst, schur)
 

time: 276 us -> 290 us (1.051)
  starting transfers between devices: 0.08 us -> 10.2 us
  blocking collectives: 30.7 us -> 37.9 us
  waiting for transfers between devices: 162 us -> 158 us
    psum x1 -> x0, waiting for transfers between devices: 36.6 us -> none  [local(): total = lax.psum(owned, 'cont')]
    ppermute x0 -> x3, waiting for transfers between devices: none -> 32.3 us  [local(): lax.ppermute(total, 'cont', [(dev, dev ^ hop) for dev in range(8)])]
    ppermute x0 -> x3, starting transfers between devices: none -> 10.1 us  [local(): lax.ppermute(total, 'cont', [(dev, dev ^ hop) for dev in range(8)])]
    pmax x1, blocking collectives: 30.7 us -> 37.9 us  [local(): worst = lax.pmax(local_worst, 'cont') / limits[:, None]]
  transfers between devices with their start and end apart: 2 -> 4, of which waited for: 2 -> 3; matrix products, arithmetic and copies ran while one was open for 3% -> 3% of each run, Pallas kernels for 0% -> 0%
where the time goes in v1:
time: 290 us; the launch traced here: 289 us
  waiting for transfers between devices  158 us (54%)
  blocking collectives  37.9 us (13%)
  local copies, waits for them, and re-layouts  32.1 us (11%)
  other arithmetic  18.5 us (6%)
  matrix products  17.3 us (6%)
  between operations  15 us (5%)
  starting transfers between devices  10.2 us (4%)
    reduce_scatter x1, waiting for transfers between devices, local(): lax.psum_scatter(lax.fori_loop(0, trips, step, jnp.zeros((lax.axis_size((...  126 us
    pmax x1, blocking collectives, local(): worst = lax.pmax(local_worst, 'cont') / limits[:, None]  37.9 us
    ppermute x3, waiting for transfers between devices, local(): lax.ppermute(total, 'cont', [(dev, dev ^ hop) for dev in range(8)])  32.3 us
    dot_general x1, matrix products, step(): lax.dot_general(row_tile, scaled_tile, (((0,), (0,)), ((), ())), preferre...  17.3 us
    ppermute x3, starting transfers between devices, local(): lax.ppermute(total, 'cont', [(dev, dev ^ hop) for dev in range(8)])  10.1 us
    gather x2, local copies, waits for them, and re-layouts, local(): post = flow[viol_line, viol_scen] + coef * out_flow[viol_scen, viol_cont]  8.27 us
    broadcast_in_dim x1, local copies, waits for them, and re-layouts, local(): jnp.zeros((lax.axis_size(('line', 'scen')) * (width // owners), width), j...  7.86 us
  transfers between devices with their start and end apart: 4, of which 3 were waited for; matrix products, arithmetic and copies ran while one was open for 3% of the time, Pallas kernels for 0%

profile of v1, /device:TPU:2, one launch (start us, length us, event | category | flops | bytes accessed | tf_op | source)
XLA Modules:
  0.0 289.3 jit_solution(11037322101690842595)
XLA Ops:
  8.8 5.2 %gather_fusion.1 = bf16[512]{0:T(512)(128)(2,1)S(1)} fusion(bf16[128,512]{1,0:T(8,128)(2,1)} %param.14, s32[512]{0:T(512)S(1)} %get-tuple-element.84), kind=kCustom, calls=%fused_computation.1 | custom fusion | bytes 6144 | tf_op jit(solution)/shard_map/gather | solution.py:39
  14.0 3.4 %gather_fusion = bf16[512,2048]{1,0:T(8,128)(2,1)} fusion(bf16[128,2048]{1,0:T(8,128)(2,1)S(1)} %copy-done.2, s32[1024]{0:T(1024)S(1)} %get-tuple-element.89), kind=kCustom, calls=%fused_computation | custom fusion | bytes 4196352 | tf_op jit(solution)/shard_map/gather | solution.py:41
  17.3 3.3 %gather_fusion.2 = bf16[512,2048]{1,0:T(8,128)(2,1)} fusion(bf16[512,2048]{1,0:T(8,128)(2,1)S(1)} %copy-done, s32[1024]{0:T(1024)S(1)} %get-tuple-element.88), kind=kCustom, calls=%fused_computation.2 | custom fusion | bytes 4196352 | tf_op jit(solution)/shard_map/gather | solution.py:42
  20.6 4.2 %add_convert_fusion = bf16[512,2048]{1,0:T(8,128)(2,1)} fusion(bf16[512,2048]{1,0:T(8,128)(2,1)} %gather_fusion.2, bf16[512,2048]{1,0:T(8,128)(2,1)} %gather_fusion, f32[512]{0:T(512)S(1)} %convert_element_type.36), kind=kLoop, calls=%fused_computation.14 | loop fusion | flops 5242880 | bytes 6293504 | tf_op jit(solution)/shard_map/convert_element_type | solution.py:43
  24.9 3.3 %gather_fusion.5 = f32[512]{0:T(512)S(1)} fusion(f32[128]{0:T(128)S(1)} %copy-done.1, s32[1024]{0:T(1024)S(1)} %get-tuple-element.89), kind=kCustom, calls=%fused_computation.5 | custom fusion | bytes 6144 | tf_op jit(solution)/shard_map/gather | solution.py:46
  28.2 3.7 %gather_fusion.3 = f32[512]{0:T(512)S(1)} fusion(f32[128,64]{0,1:T(8,128)S(1)} %copy-done.3, s32[512]{0:T(512)S(1)} %get-tuple-element.85), kind=kCustom, calls=%fused_computation.3 | custom fusion | bytes 8192 | tf_op jit(solution)/shard_map/gather | solution.py:45
  32.0 4.5 %gather_fusion.4 = f32[512]{0:T(512)S(1)} fusion(f32[64,512]{1,0:T(8,128)S(1)} %copy-done.4, s32[512]{0:T(512)S(1)} %get-tuple-element.83), kind=kCustom, calls=%fused_computation.4 | custom fusion | bytes 8192 | tf_op jit(solution)/shard_map/gather | solution.py:45
  36.5 3.4 %fusion.2 = bf16[1,512,2048]{2,1,0:T(8,128)(2,1)} fusion(bf16[512,2048]{1,0:T(8,128)(2,1)} %add_convert_fusion, f32[512]{0:T(512)S(1)} %add_select_fusion), kind=kLoop, calls=%fused_computation.15 | loop fusion | flops 3145728 | bytes 4196352 | tf_op jit(solution)/shard_map/reshape | solution.py:52
  39.9 7.9 %broadcast_in_dim.20 = f32[2048,2048]{1,0:T(8,128)} broadcast(f32[]{:T(128)} %constant.46.clone.1), dimensions={} | broadcast | bytes 16777220 | tf_op jit(solution)/shard_map/broadcast_in_dim | solution.py:66
  47.8 17.3 %while.21 = (s32[]{:T(128)}, f32[2048,2048]{1,0:T(8,128)}, s32[]{:T(128)}, bf16[1,512,2048]{2,1,0:T(8,128)(2,1)}, bf16[1,512,2048]{2,1,0:T(8,128)(2,1)}, /*index=5*/s32[]{:T(128)}) while((s32[]{:T(128)}, f32[2048,2048]{1,0:T(8,128)}, s32[]{:T(128)}, bf16[1,512,2048]{2,1,0:T(8,128)(2,1)}, bf16[1,512,2048]{2,1,0:T(8,128)(2,1)}, ...), condition=%wide.region_5.6_spmd, body=%wide.region_4.5_spmd.sunk | while | flops 4299161600 | bytes 37748804 | solution.py:62
  47.8 17.3 %convolution_add_fusion.2 = f32[2048,2048]{1,0:T(8,128)} fusion(f32[2048,2048]{1,0:T(8,128)} %get-tuple-element.178, bf16[1,512,2048]{2,1,0:T(8,128)(2,1)} %get-tuple-element.187, bf16[1,512,2048]{2,1,0:T(8,128)(2,1)} %get-tuple-element.186), kind=kOutput, calls=%fused_computation.10.clone.1 | convolution fusion | flops 4299161600 | bytes 37748736 | tf_op jit(solution)/shard_map/while/body/dot_general | solution.py:57
  65.1 125.9 %reduce-scatter.2.cloned.1.call-done = f32[64,2048]{1,0:T(8,128)} async-done(((f32[2048,2048]{1,0:T(8,128)}), f32[64,2048]{1,0:T(8,128)}) %reduce-scatter.2.cloned.1.call-update) | async-done | bytes 524304 | tf_op jit(solution)/shard_map/reduce_scatter | solution.py:61
  191.0 1.5 collective-permute-start
  192.5 11.2 %collective-permute-done = f32[64,2048]{1,0:T(8,128)S(1)} collective-permute-done((f32[64,2048]{1,0:T(8,128)}, f32[64,2048]{1,0:T(8,128)S(1)}, u32[]{:S(2)}, u32[]{:S(2)}) %collective-permute-start) | collective-permute-done | bytes 524320 | tf_op jit(solution)/shard_map/ppermute | solution.py:74
  203.7 1.1 add.80
  204.8 2.7 collective-permute-start.1
  207.6 21.1 %collective-permute-done.1 = f32[64,2048]{1,0:T(8,128)} collective-permute-done((f32[64,2048]{1,0:T(8,128)S(1)}, f32[64,2048]{1,0:T(8,128)}, u32[]{:S(2)}, u32[]{:S(2)}) %collective-permute-start.1) | collective-permute-done | bytes 524320 | tf_op jit(solution)/shard_map/ppermute | solution.py:74
  228.8 1.1 add.81
  229.9 5.9 %collective-permute-start.2 = (f32[64,2048]{1,0:T(8,128)S(1)}, f32[64,2048]{1,0:T(8,128)S(1)}, u32[]{:S(2)}, u32[]{:S(2)}) collective-permute-start(f32[64,2048]{1,0:T(8,128)S(1)} %add.81), channel_id=1, source_target_pairs={{0,128},{32,160},{64,192},{96,224},{128,0},{160,32},{192,64},{224,... | collective-permute-start | bytes 1572872 | tf_op jit(solution)/shard_map/ppermute | solution.py:74
  235.8 7.1 %while.20 = (s32[]{:T(128)}, f32[4,32,64]{2,1,0:T(8,128)S(1)}, f32[4,32,64]{2,1,0:T(8,128)S(1)}, bf16[4,32,512]{2,1,0:T(8,128)(2,1)}, f32[64,512]{1,0:T(8,128)S(1)}, /*index=5*/s32[]{:T(128)}) while((s32[]{:T(128)}, f32[4,32,64]{2,1,0:T(8,128)S(1)}, f32[4,32,64]{2,1,0:T(8,128)S(1)}, bf16[4,32,512]{2,1,0:T(8,128)(2,1)}, ...), condition=%wide.region_2.3_spmd, body=%wide.region_0.2_spmd.sunk | while | flops 4208642 | bytes 360529 | solution.py:31
  236.6 1.0 abs_reduce_fusion.2
  238.4 1.0 abs_reduce_fusion.2
  240.1 1.0 abs_reduce_fusion.2
  242.9 37.9 %pmax.7 = f32[128,64]{1,0:T(8,128)S(1)} all-reduce(f32[128,64]{1,0:T(8,128)S(1)} %bitcast.35), channel_id=1, replica_groups=mesh['cont'=8,'line'=8,'scen'=4] {'cont'}, use_global_device_ids=true, to_apply=%region_3.4 | all-reduce | flops 8192 | bytes 65536 | tf_op jit(solution)/shard_map/pmax | solution.py:38
  (35 shorter events, 6.6 us)
Async XLA Ops:
  7.2 10.2 %copy-start = (bf16[512,2048]{1,0:T(8,128)(2,1)S(1)}, bf16[512,2048]{1,0:T(8,128)(2,1)}, u32[]{:S(2)}) copy-start(bf16[512,2048]{1,0:T(8,128)(2,1)} %param.19) | copy-start | bytes 6291460
  7.2 6.8 %copy-start.2 = (bf16[128,2048]{1,0:T(8,128)(2,1)S(1)}, bf16[128,2048]{1,0:T(8,128)(2,1)}, u32[]{:S(2)}) copy-start(bf16[128,2048]{1,0:T(8,128)(2,1)} %param.18) | copy-start | bytes 1572868
  7.2 183.8 %reduce-scatter.2.cloned.1.call-start = ((), (), s32[]{:S(2)}) async-start(), calls=%async_computation.1 | async-start | bytes 17301504 | tf_op jit(solution)/shard_map/reduce_scatter | solution.py:61
  20.6 4.2 %copy-start.1 = (f32[128]{0:T(128)S(1)}, f32[128]{0:T(128)}, u32[]{:S(2)}) copy-start(f32[128]{0:T(128)} %param.17) | copy-start | bytes 1540
  24.9 3.4 %copy-start.3 = (f32[128,64]{0,1:T(8,128)S(1)}, f32[128,64]{0,1:T(8,128)}, u32[]{:S(2)}) copy-start(f32[128,64]{0,1:T(8,128)} %param.15) | copy-start | bytes 98308
  24.9 7.1 %copy-start.4 = (f32[64,512]{1,0:T(8,128)S(1)}, f32[64,512]{1,0:T(8,128)}, u32[]{:S(2)}) copy-start(f32[64,512]{1,0:T(8,128)} %param.16) | copy-start | bytes 393220
  191.0 12.7 %collective-permute-start = (f32[64,2048]{1,0:T(8,128)}, f32[64,2048]{1,0:T(8,128)S(1)}, u32[]{:S(2)}, u32[]{:S(2)}) collective-permute-start(f32[64,2048]{1,0:T(8,128)} %reduce-scatter.2.cloned.1.call-done), channel_id=1, source_target_pairs={{0,32},{32,0},{64,96},{96,64},{128,160},{160,128},{192,224},{224,1... | collective-permute-start | bytes 1572872 | tf_op jit(solution)/shard_map/ppermute | solution.py:74
  204.8 23.9 %collective-permute-start.1 = (f32[64,2048]{1,0:T(8,128)S(1)}, f32[64,2048]{1,0:T(8,128)}, u32[]{:S(2)}, u32[]{:S(2)}) collective-permute-start(f32[64,2048]{1,0:T(8,128)S(1)} %add.80), channel_id=1, source_target_pairs={{0,64},{32,96},{64,0},{96,32},{128,192},{160,224},{192,128},{224,1... | collective-permute-start | bytes 1572872 | tf_op jit(solution)/shard_map/ppermute | solution.py:74
  229.9 51.7 %collective-permute-start.2 = (f32[64,2048]{1,0:T(8,128)S(1)}, f32[64,2048]{1,0:T(8,128)S(1)}, u32[]{:S(2)}, u32[]{:S(2)}) collective-permute-start(f32[64,2048]{1,0:T(8,128)S(1)} %add.81), channel_id=1, source_target_pairs={{0,128},{32,160},{64,192},{96,224},{128,0},{160,32},{192,64},{224,... | collective-permute-start | bytes 1572872 | tf_op jit(solution)/shard_map/ppermute | solution.py:74
Sparse Core Ops, SparseCore 0:
  65.3 125.7 reduce-scatter.1
